TPU v7x, 256 devices: a whole 4x4x8 slice. The times are simulated.
256 devices in a mesh: dp: 4 (over z_hi), graph: 64 (over y, z_lo, x, core).
Axes of the slice: x: 4, y: 4, z: 8 (z_hi: 4, z_lo: 2; z = z_hi * 2 + z_lo), core: 2. Of those that a mesh axis runs over, the one named last changes fastest.
Arguments:
- inputs: bfloat16 [4, 32768, 256], P('dp', 'graph')
- gain: float32 [256], replicated, may hold values from 0.25 to 1.75
- w_query: bfloat16 [256, 256], replicated
- w_key: bfloat16 [256, 256], replicated
- w_value: bfloat16 [256, 256], replicated, may hold values from -0.375 to 0.375
- w_out: bfloat16 [256, 256], replicated, may hold values from -0.375 to 0.375
- block_slots: int32 [32768], P('graph'), may hold values from 0 to 32767, as said below
- matchings: int32 [4, 128], replicated, may hold values from 0 to 127, as said below
- cotangent: bfloat16 [4, 32768, 256], P('dp', 'graph'), may hold values from -6 to 6
Outputs:
- update: bfloat16 [4, 32768, 256], P('dp', 'graph')
- grad_inputs: bfloat16 [4, 32768, 256], P('dp', 'graph')
- grad_query: float32 [256, 256], replicated
- grad_key: float32 [256, 256], replicated
- grad_value: float32 [256, 256], replicated
- grad_out: float32 [256, 256], replicated
- grad_gain: float32 [256], replicated
Inputs may be any that keep to these rules, and one draw needn't show every extreme that they name: `block_slots`: each graph index's 2 * 256 slots hold a permutation of that index's own sensors. `matchings`: each row is an involution of the blocks without fixed points. Block b lives on graph index b // 2; in matching r the partner of every block on index i lives on index i XOR 2 ** ((r * log2(64)) // 4).
All inputs are finite; a program needn't handle non-finite values.
Results may differ from a plain program's by a relative error of at most 0.02.
The roundings to bfloat16 on the way count: a program that leaves them out, or rounds other values in their place, can miss the bound.
Values may be sent and summed in bfloat16 or wider, within the bound.
A program may use at most 64 MiB of HBM per device.

v0:
```python
import jax
import jax.numpy as jnp
from jax import lax
from jax.sharding import PartitionSpec as P

HEADS = 8


epsilon = 1e-06


def swapped(block, axis, distance):
    count = lax.axis_size(axis)
    route = []
    for low in range(count):
        high = low | 1 << distance
        if high != low and high < count:
            route += [(low, high), (high, low)]
    return lax.ppermute(block, axis, route)


def to_heads(array):
    wins, blocks, count, feature = array.shape
    return array.reshape(wins, blocks, count, HEADS, feature // HEADS).transpose(3, 0, 1, 2, 4)


def from_heads(array):
    heads, wins, blocks, count, head_dim = array.shape
    return array.transpose(1, 2, 3, 0, 4).reshape(wins, blocks, count, heads * head_dim)


def head_scores(query_head, key_head, score_scale):
    return (
        jnp.einsum("wbqe,wbke->wbqk", query_head, key_head, preferred_element_type=jnp.float32)
        * score_scale
    )


def head_forward(query_head, key_head, value_head, score_scale):
    scores = head_scores(query_head, key_head, score_scale)
    row_max = jnp.max(scores, axis=-1, keepdims=True)
    expo = jnp.exp(scores - row_max)
    row_sum = jnp.sum(expo, axis=-1, keepdims=True)
    weights = (expo / row_sum).astype(jnp.bfloat16)
    attended = jnp.einsum(
        "wbqk,wbke->wbqe", weights, value_head, preferred_element_type=jnp.float32
    )
    return (attended.astype(jnp.bfloat16), row_max[..., 0], row_sum[..., 0])


def head_backward(query_head, key_head, value_head, grad_head, row_max, row_sum, score_scale):
    scores = head_scores(query_head, key_head, score_scale)
    probs = jnp.exp(scores - row_max[..., None]) / row_sum[..., None]
    weights = probs.astype(jnp.bfloat16)
    prob_grad = jnp.einsum(
        "wbqe,wbke->wbqk", grad_head, value_head, preferred_element_type=jnp.float32
    )
    row_dot = jnp.sum(prob_grad * probs, axis=-1)
    score_grad = (probs * (prob_grad - row_dot[..., None])).astype(jnp.bfloat16)
    value_part = jnp.einsum(
        "wbqk,wbqe->wbke", weights, grad_head, preferred_element_type=jnp.float32
    )
    query_part = (
        jnp.einsum("wbqk,wbke->wbqe", score_grad, key_head, preferred_element_type=jnp.float32)
        * score_scale
    )
    key_part = (
        jnp.einsum("wbqk,wbqe->wbke", score_grad, query_head, preferred_element_type=jnp.float32)
        * score_scale
    )
    return (query_part, key_part, value_part, row_dot)


def local(inputs, gain, w_query, w_key, w_value, w_out, block_slots, matchings, cotangent):
    graph_index = lax.axis_index("graph")
    graph_count = lax.axis_size("graph")
    nbits = graph_count.bit_length() - 1
    rounds = matchings.shape[0]
    blocks_dev = matchings.shape[1] // graph_count
    windows, sens_dev, model_width = inputs.shape
    span = sens_dev // blocks_dev
    score_scale = (model_width // HEADS) ** (-0.5)
    local_slots = block_slots - graph_index * sens_dev
    slotted = jnp.take(inputs, local_slots, axis=1)
    slot_f = slotted.astype(jnp.float32)
    inv_rms = lax.rsqrt(jnp.mean(slot_f * slot_f, axis=-1, keepdims=True) + epsilon)
    normed = (slot_f * inv_rms * gain).astype(jnp.bfloat16)
    norm_rows = normed.reshape(-1, model_width)

    def project(weight):
        out = jnp.dot(norm_rows, weight, preferred_element_type=jnp.float32).astype(jnp.bfloat16)
        return out.reshape(windows, blocks_dev, span, model_width)

    queries = project(w_query)
    keys_own = project(w_key)
    values_own = project(w_value)
    bit_list = []
    pair_list = []
    for turn in range(rounds):
        bit_pos = turn * nbits // rounds
        partner = jnp.bitwise_xor(graph_index, 1 << bit_pos)
        mine = lax.dynamic_slice_in_dim(matchings[turn], graph_index * blocks_dev, blocks_dev)
        bit_list.append(bit_pos)
        pair_list.append(mine - partner * blocks_dev)
    far_keys = []
    far_values = []
    for turn in range(rounds):
        got_keys, got_values = swapped((keys_own, values_own), "graph", bit_list[turn])
        far_keys.append(jnp.take(got_keys, pair_list[turn], axis=1))
        far_values.append(jnp.take(got_values, pair_list[turn], axis=1))
    query_heads = to_heads(queries)
    key_heads = to_heads(jnp.concatenate([keys_own] + far_keys, axis=2))
    value_heads = to_heads(jnp.concatenate([values_own] + far_values, axis=2))
    att_heads, row_max, row_sum = lax.map(
        lambda parts: head_forward(parts[0], parts[1], parts[2], score_scale),
        (query_heads, key_heads, value_heads),
    )
    att_rows = from_heads(att_heads).reshape(-1, model_width)
    update_rows = jnp.dot(att_rows, w_out, preferred_element_type=jnp.float32).astype(jnp.bfloat16)
    update = (
        jnp.zeros_like(inputs)
        .at[:, local_slots]
        .set(update_rows.reshape(windows, sens_dev, model_width))
    )
    cot_rows = jnp.take(cotangent, local_slots, axis=1).reshape(-1, model_width)
    grad_out = jnp.dot(att_rows.T, cot_rows, preferred_element_type=jnp.float32)
    out_grad = jnp.dot(cot_rows, w_out.T, preferred_element_type=jnp.float32).astype(jnp.bfloat16)
    out_grad = out_grad.reshape(windows, blocks_dev, span, model_width)
    again_keys = []
    again_values = []
    for turn in range(rounds):
        got_keys, got_values = swapped((keys_own, values_own), "graph", bit_list[turn])
        again_keys.append(jnp.take(got_keys, pair_list[turn], axis=1))
        again_values.append(jnp.take(got_values, pair_list[turn], axis=1))
    back_keys = to_heads(jnp.concatenate([keys_own] + again_keys, axis=2))
    back_values = to_heads(jnp.concatenate([values_own] + again_values, axis=2))
    grad_heads = to_heads(out_grad)
    query_part, key_part, value_part, row_dot = lax.map(
        lambda parts: head_backward(
            parts[0], parts[1], parts[2], parts[3], parts[4], parts[5], score_scale
        ),
        (query_heads, back_keys, back_values, grad_heads, row_max, row_sum),
    )
    key_all = from_heads(key_part)
    value_all = from_heads(value_part)
    key_total = key_all[:, :, :span]
    value_total = value_all[:, :, :span]
    for turn in range(rounds):
        back_order = jnp.argsort(pair_list[turn])
        send_keys = jnp.take(
            key_all[:, :, (turn + 1) * span : (turn + 2) * span], back_order, axis=1
        )
        send_values = jnp.take(
            value_all[:, :, (turn + 1) * span : (turn + 2) * span], back_order, axis=1
        )
        got_keys, got_values = (
            swapped(send_keys.astype(jnp.bfloat16), "graph", bit_list[turn]).astype(
                send_keys.dtype
            ),
            swapped(send_values.astype(jnp.bfloat16), "graph", bit_list[turn]).astype(
                send_values.dtype
            ),
        )
        key_total = key_total + got_keys
        value_total = value_total + got_values
    query_grad = from_heads(query_part).reshape(-1, model_width).astype(jnp.bfloat16)
    key_grad = key_total.reshape(-1, model_width).astype(jnp.bfloat16)
    value_grad = value_total.reshape(-1, model_width).astype(jnp.bfloat16)
    grad_query = jnp.dot(norm_rows.T, query_grad, preferred_element_type=jnp.float32)
    grad_key = jnp.dot(norm_rows.T, key_grad, preferred_element_type=jnp.float32)
    grad_value = jnp.dot(norm_rows.T, value_grad, preferred_element_type=jnp.float32)
    normed_grad = jnp.dot(query_grad, w_query.T, preferred_element_type=jnp.float32)
    normed_grad = normed_grad + jnp.dot(key_grad, w_key.T, preferred_element_type=jnp.float32)
    normed_grad = normed_grad + jnp.dot(value_grad, w_value.T, preferred_element_type=jnp.float32)
    normed_grad = normed_grad.reshape(windows, sens_dev, model_width)
    grad_gain = jnp.sum(normed_grad * slot_f * inv_rms, axis=(0, 1))
    scaled = normed_grad * gain
    slot_grad = inv_rms * scaled - slot_f * (inv_rms * inv_rms * inv_rms) * jnp.mean(
        slot_f * scaled, axis=-1, keepdims=True
    )
    grad_inputs = jnp.zeros_like(inputs).at[:, local_slots].set(slot_grad.astype(jnp.bfloat16))
    summed = lax.psum((grad_query, grad_key, grad_value, grad_out, grad_gain), ("dp", "graph"))
    return (update, grad_inputs, summed[0], summed[1], summed[2], summed[3], summed[4])


def solution(mesh):
    placed = (
        P("dp", "graph", None),
        P(),
        P(),
        P(),
        P(),
        P(),
        P("graph"),
        P(),
        P("dp", "graph", None),
    )
    return jax.shard_map(
        local,
        mesh=mesh,
        in_specs=placed,
        out_specs=(P("dp", "graph", None), P("dp", "graph", None), P(), P(), P(), P(), P()),
        check_vma=False,
    )
```

profile of v0, /device:TPU:1, one launch (start us, length us, event | category | flops | bytes accessed | tf_op | source)
XLA Modules:
  0.0 473.6 jit_solution(11280498359730881664)
XLA Ops:
  8.1 1.9 gather_fusion
  11.4 2.1 collective-permute-start.7
  13.5 1.6 collective-permute-start.6
  28.7 1.9 gather_fusion.9
  36.7 2.2 collective-permute-start.4
  39.7 1.8 collective-permute-start.1
  41.5 1.6 gather_fusion.4
  45.2 1.6 gather_fusion.3
  46.8 1.4 bitcast_select_fusion.10
  49.2 1.8 copy.56
  51.1 1.6 gather_fusion.6
  52.8 1.6 gather_fusion.2
  54.4 1.4 bitcast_select_fusion.11
  55.8 1.8 copy.55
  57.8 1.6 gather_fusion.5
  59.4 1.6 gather_fusion.1
  61.1 1.6 bitcast_select_fusion.12
  62.6 1.8 copy.54
  69.6 1.6 copy.63
  73.8 1.5 copy.64
  75.3 24.8 %while.28 = (s32[]{:T(128)}, bf16[8,1,2,256,32]{3,4,2,1,0:T(8,128)(2,1)}, f32[8,1,2,256]{3,2,1,0:T(2,128)}, f32[8,1,2,256]{3,2,1,0:T(2,128)}, bf16[8,1,2,256,32]...) while((s32[]{:T(128)}, ...), condition=%wide.region_4.7_spmd, body=%wide.region_1.6_spmd.sunk | while | flops 88488960 | bytes 8278113 | solution.py:114
  76.5 1.3 fusion.141
  79.6 1.3 fusion.141
  82.7 1.3 fusion.141
  85.8 1.3 fusion.141
  88.9 1.3 fusion.141
  92.0 1.3 fusion.141
  95.1 1.3 fusion.141
  98.2 1.3 fusion.141
  100.1 1.3 copy.65
  101.5 2.0 fusion.68
  103.5 62.7 %while.29 = (s32[]{:T(128)}, bf16[8,1,2,256,32]{3,4,2,1,0:T(8,128)(2,1)}, f32[8,1,2,1280,32]{3,4,0,2,1:T(8,128)}, f32[8,1,2,1280,32]{3,4,0,2,1:T(8,128)}, bf16[8...) while((s32[]{:T(128)}, ...), condition=%wide.region_8.11_spmd, body=%wide.region_6.10_spmd.sunk | while | flops 215711232 | bytes 21089412 | solution.py:138
  104.9 1.5 fusion.150
  109.5 1.8 fusion.152
  112.8 1.5 fusion.150
  117.3 1.8 fusion.152
  120.6 1.5 fusion.150
  125.2 1.8 fusion.152
  128.4 1.5 fusion.150
  133.0 1.8 fusion.152
  136.3 1.5 fusion.150
  140.8 1.8 fusion.152
  144.1 1.5 fusion.150
  148.7 1.8 fusion.152
  152.0 1.5 fusion.150
  156.5 1.8 fusion.152
  159.8 1.5 fusion.150
  164.4 1.8 fusion.152
  167.5 1.8 fusion.92
  169.3 1.6 slice_bitcast_fusion.3
  170.9 1.6 slice_bitcast_fusion.7
  178.1 1.5 fusion.58
  180.0 1.6 fusion.57
  183.4 1.3 collective-permute-start.15
  187.7 3.0 scatter_custom_fusion
  192.0 1.4 collective-permute-start.11
  196.7 3.1 collective-permute-done.10
  199.9 1.3 fusion.55
  203.8 3.3 scatter_custom_fusion.1
  207.1 79.5 %psum.39 = f32[256]{0:T(256)} all-reduce(f32[256]{0:T(256)S(1)} %get-tuple-element.151), channel_id=1, replica_groups=mesh['dp'=4,'graph'=64] {'dp','graph'}, use_global_device_ids=true, to_apply=%region_20.24 | all-reduce | flops 256 | bytes 2048 | tf_op jit(solution)/shard_map/psum | solution.py:182
  286.6 174.3 %all-reduce.3.cloned.1.call-done = (f32[256,256]{1,0:T(8,128)}, f32[256,256]{1,0:T(8,128)}, f32[256,256]{1,0:T(8,128)}, f32[256,256]{1,0:T(8,128)}) async-done(((f32[256,256]{1,0:T(8,128)}, f32[256,256]{1,0:T(8,128)}, f32[256,256]{1,0:T(8,128)}, f32[256,256]{1,0:T(8,128)}), (f32[256,256]{1,0:T(8,128)}, f32[256,256]{1,0:T(8,128)}, f32[256,256]{1,0:T(8,128)}, ...) | async-done | bytes 1048592 | tf_op jit(solution)/shard_map/psum | solution.py:182
  461.0 1.7 copy.147
  462.7 1.7 copy.148
  464.3 1.7 copy.149
  (237 shorter events, 103.7 us)
Async XLA Ops:
  7.2 1.0 copy-start
  7.2 453.8 %all-reduce.3.cloned.1.call-start = ((), (), s32[]{:S(2)}) async-start(), calls=%async_computation | async-start | bytes 2097152 | tf_op jit(solution)/shard_map/psum | solution.py:182
  8.1 2.2 copy-start.13
  8.1 2.2 copy-start.17
  8.1 8.3 %copy-start.15 = (bf16[256,256]{1,0:T(8,128)(2,1)S(1)}, bf16[256,256]{1,0:T(8,128)(2,1)}, u32[]{:S(2)}) copy-start(bf16[256,256]{1,0:T(8,128)(2,1)} %param.22) | copy-start | bytes 393220
  10.1 7.5 %copy-start.21 = (s32[4,128]{1,0:T(4,128)S(1)}, s32[4,128]{1,0:T(4,128)}, u32[]{:S(2)}) copy-start(s32[4,128]{1,0:T(4,128)} %param.26) | copy-start | bytes 6148
  10.3 18.4 %copy-start.1 = (bf16[1,512,256]{2,1,0:T(8,128)(2,1)S(1)}, bf16[1,512,256]{2,1,0:T(8,128)(2,1)}, u32[]{:S(2)}) copy-start(bf16[1,512,256]{2,1,0:T(8,128)(2,1)} %param.27) | copy-start | bytes 786436
  11.4 25.3 %collective-permute-start.7 = (bf16[1,2,256,256]{3,2,1,0:T(8,128)(2,1)}, bf16[1,2,256,256]{3,2,1,0:T(8,128)(2,1)S(1)}, u32[]{:S(2)}, u32[]{:S(2)}) collective-permute-start(bf16[1,2,256,256]{3,2,1,0:T(8,128)(2,1)} %bitcast.37), channel_id=1, source_target_pairs={{0,16},{16,0},{1,17},{17,1},{2,18},{18,2},{3,19},{19,3},{4,20},{20... | collective-permute-start | bytes 786440 | tf_op jit(solution)/shard_map/ppermute | solution.py:19
  13.5 30.3 %collective-permute-start.6 = (bf16[1,2,256,256]{3,2,1,0:T(8,128)(2,1)}, bf16[1,2,256,256]{3,2,1,0:T(8,128)(2,1)S(1)}, u32[]{:S(2)}, u32[]{:S(2)}) collective-permute-start(bf16[1,2,256,256]{3,2,1,0:T(8,128)(2,1)} %bitcast.37), channel_id=1, source_target_pairs={{0,8},{8,0},{1,9},{9,1},{2,10},{10,2},{3,11},{11,3},{4,12},{12,4},... | collective-permute-start | bytes 786440 | tf_op jit(solution)/shard_map/ppermute | solution.py:19
  15.2 35.9 %collective-permute-start.5 = (bf16[1,2,256,256]{3,2,1,0:T(8,128)(2,1)}, bf16[1,2,256,256]{3,2,1,0:T(8,128)(2,1)}, u32[]{:S(2)}, u32[]{:S(2)}) collective-permute-start(bf16[1,2,256,256]{3,2,1,0:T(8,128)(2,1)} %bitcast.37), channel_id=1, source_target_pairs={{0,2},{2,0},{1,3},{3,1},{4,6},{6,4},{5,7},{7,5},{8,10},{10,8},{9,1... | collective-permute-start | bytes 786440 | tf_op jit(solution)/shard_map/ppermute | solution.py:19
  17.4 22.2 %collective-permute-start.3 = (bf16[1,2,256,256]{3,2,1,0:T(8,128)(2,1)}, bf16[1,2,256,256]{3,2,1,0:T(8,128)(2,1)S(1)}, u32[]{:S(2)}, u32[]{:S(2)}) collective-permute-start(bf16[1,2,256,256]{3,2,1,0:T(8,128)(2,1)} %bitcast.20), channel_id=1, source_target_pairs={{0,16},{16,0},{1,17},{17,1},{2,18},{18,2},{3,19},{19,3},{4,20},{20... | collective-permute-start | bytes 786440 | tf_op jit(solution)/shard_map/ppermute | solution.py:19
  17.6 27.6 %collective-permute-start.2 = (bf16[1,2,256,256]{3,2,1,0:T(8,128)(2,1)}, bf16[1,2,256,256]{3,2,1,0:T(8,128)(2,1)}, u32[]{:S(2)}, u32[]{:S(2)}) collective-permute-start(bf16[1,2,256,256]{3,2,1,0:T(8,128)(2,1)} %bitcast.20), channel_id=1, source_target_pairs={{0,8},{8,0},{1,9},{9,1},{2,10},{10,2},{3,11},{11,3},{4,12},{12,4},... | collective-permute-start | bytes 786440 | tf_op jit(solution)/shard_map/ppermute | solution.py:19
  28.7 2.1 copy-start.12
  30.7 1.7 copy-start.8
  30.7 1.4 copy-start.11
  36.7 21.0 %collective-permute-start.4 = (bf16[1,2,256,256]{3,2,1,0:T(8,128)(2,1)}, bf16[1,2,256,256]{3,2,1,0:T(8,128)(2,1)}, u32[]{:S(2)}, u32[]{:S(2)}) collective-permute-start(bf16[1,2,256,256]{3,2,1,0:T(8,128)(2,1)} %bitcast.37), channel_id=1, source_target_pairs={{0,1},{1,0},{2,3},{3,2},{4,5},{5,4},{6,7},{7,6},{8,9},{9,8},{10,11... | collective-permute-start | bytes 786440 | tf_op jit(solution)/shard_map/ppermute | solution.py:19
  39.6 1.8 copy-start.9
  39.7 13.1 %collective-permute-start.1 = (bf16[1,2,256,256]{3,2,1,0:T(8,128)(2,1)}, bf16[1,2,256,256]{3,2,1,0:T(8,128)(2,1)}, u32[]{:S(2)}, u32[]{:S(2)}) collective-permute-start(bf16[1,2,256,256]{3,2,1,0:T(8,128)(2,1)} %bitcast.20), channel_id=1, source_target_pairs={{0,2},{2,0},{1,3},{3,1},{4,6},{6,4},{5,7},{7,5},{8,10},{10,8},{9,1... | collective-permute-start | bytes 786440 | tf_op jit(solution)/shard_map/ppermute | solution.py:19
  43.9 15.5 %collective-permute-start = (bf16[1,2,256,256]{3,2,1,0:T(8,128)(2,1)}, bf16[1,2,256,256]{3,2,1,0:T(8,128)(2,1)}, u32[]{:S(2)}, u32[]{:S(2)}) collective-permute-start(bf16[1,2,256,256]{3,2,1,0:T(8,128)(2,1)} %bitcast.20), channel_id=1, source_target_pairs={{0,1},{1,0},{2,3},{3,2},{4,5},{5,4},{6,7},{7,6},{8,9},{9,8},{10,11... | collective-permute-start | bytes 786440 | tf_op jit(solution)/shard_map/ppermute | solution.py:19
  69.6 1.6 copy-start.7
  69.6 2.0 copy-start.6
  69.6 2.4 copy-start.5
  71.2 1.1 copy-start.4
  72.7 1.1 copy-start.2
  100.1 1.3 copy-start.3
  178.1 4.3 copy-start.19
  179.6 5.0 %copy-start.20 = (pred[2]{0:T(512)(128)(4,1)S(1)}, pred[2]{0:T(512)(128)(4,1)}, u32[]{:S(2)}) copy-start(pred[2]{0:T(512)(128)(4,1)} %get-tuple-element.247) | copy-start | bytes 10
  179.6 12.2 %collective-permute-start.13 = (bf16[1,2,256,256]{2,3,1,0:T(8,128)(2,1)S(1)}, bf16[1,2,256,256]{2,3,1,0:T(8,128)(2,1)S(1)}, u32[]{:S(2)}, u32[]{:S(2)}) collective-permute-start(bf16[1,2,256,256]{2,3,1,0:T(8,128)(2,1)S(1)} %get-tuple-element.225), channel_id=1, source_target_pairs={{0,2},{2,0},{1,3},{3,1},{4,6},{6,4},{5,7},{7,5},{8,10},{10,8},{9,1... | collective-permute-start | bytes 786440 | tf_op jit(solution)/shard_map/ppermute | solution.py:19
  181.6 10.4 %collective-permute-start.14 = (bf16[1,2,256,256]{2,3,1,0:T(8,128)(2,1)}, bf16[1,2,256,256]{2,3,1,0:T(8,128)(2,1)S(1)}, u32[]{:S(2)}, u32[]{:S(2)}) collective-permute-start(bf16[1,2,256,256]{2,3,1,0:T(8,128)(2,1)} %get-tuple-element.227), channel_id=1, source_target_pairs={{0,8},{8,0},{1,9},{9,1},{2,10},{10,2},{3,11},{11,3},{4,12},{12,4},... | collective-permute-start | bytes 786440 | tf_op jit(solution)/shard_map/ppermute | solution.py:19
  183.4 10.0 %collective-permute-start.15 = (bf16[1,2,256,256]{2,3,1,0:T(8,128)(2,1)}, bf16[1,2,256,256]{2,3,1,0:T(8,128)(2,1)S(1)}, u32[]{:S(2)}, u32[]{:S(2)}) collective-permute-start(bf16[1,2,256,256]{2,3,1,0:T(8,128)(2,1)} %get-tuple-element.229), channel_id=1, source_target_pairs={{0,16},{16,0},{1,17},{17,1},{2,18},{18,2},{3,19},{19,3},{4,20},{20... | collective-permute-start | bytes 786440 | tf_op jit(solution)/shard_map/ppermute | solution.py:19
  185.7 8.5 %collective-permute-start.12 = (bf16[1,2,256,256]{2,3,1,0:T(8,128)(2,1)}, bf16[1,2,256,256]{2,3,1,0:T(8,128)(2,1)S(1)}, u32[]{:S(2)}, u32[]{:S(2)}) collective-permute-start(bf16[1,2,256,256]{2,3,1,0:T(8,128)(2,1)} %get-tuple-element.223), channel_id=1, source_target_pairs={{0,1},{1,0},{2,3},{3,2},{4,5},{5,4},{6,7},{7,6},{8,9},{9,8},{10,11... | collective-permute-start | bytes 786440 | tf_op jit(solution)/shard_map/ppermute | solution.py:19
  187.0 9.7 %collective-permute-start.9 = (bf16[1,2,256,256]{2,3,1,0:T(8,128)(2,1)}, bf16[1,2,256,256]{2,3,1,0:T(8,128)(2,1)S(1)}, u32[]{:S(2)}, u32[]{:S(2)}) collective-permute-start(bf16[1,2,256,256]{2,3,1,0:T(8,128)(2,1)} %get-tuple-element.226), channel_id=1, source_target_pairs={{0,2},{2,0},{1,3},{3,1},{4,6},{6,4},{5,7},{7,5},{8,10},{10,8},{9,1... | collective-permute-start | bytes 786440 | tf_op jit(solution)/shard_map/ppermute | solution.py:19
  191.9 3.7 copy-start.18
  191.9 7.9 %collective-permute-start.10 = (bf16[1,2,256,256]{2,3,1,0:T(8,128)(2,1)}, bf16[1,2,256,256]{2,3,1,0:T(8,128)(2,1)S(1)}, u32[]{:S(2)}, u32[]{:S(2)}) collective-permute-start(bf16[1,2,256,256]{2,3,1,0:T(8,128)(2,1)} %get-tuple-element.228), channel_id=1, source_target_pairs={{0,8},{8,0},{1,9},{9,1},{2,10},{10,2},{3,11},{11,3},{4,12},{12,4},... | collective-permute-start | bytes 786440 | tf_op jit(solution)/shard_map/ppermute | solution.py:19
  192.0 7.9 %collective-permute-start.11 = (bf16[1,2,256,256]{2,3,1,0:T(8,128)(2,1)}, bf16[1,2,256,256]{2,3,1,0:T(8,128)(2,1)S(1)}, u32[]{:S(2)}, u32[]{:S(2)}) collective-permute-start(bf16[1,2,256,256]{2,3,1,0:T(8,128)(2,1)} %get-tuple-element.230), channel_id=1, source_target_pairs={{0,16},{16,0},{1,17},{17,1},{2,18},{18,2},{3,19},{19,3},{4,20},{20... | collective-permute-start | bytes 786440 | tf_op jit(solution)/shard_map/ppermute | solution.py:19
  193.3 6.6 %collective-permute-start.8 = (bf16[1,2,256,256]{2,3,1,0:T(8,128)(2,1)}, bf16[1,2,256,256]{2,3,1,0:T(8,128)(2,1)}, u32[]{:S(2)}, u32[]{:S(2)}) collective-permute-start(bf16[1,2,256,256]{2,3,1,0:T(8,128)(2,1)} %get-tuple-element.224), channel_id=1, source_target_pairs={{0,1},{1,0},{2,3},{3,2},{4,5},{5,4},{6,7},{7,6},{8,9},{9,8},{10,11... | collective-permute-start | bytes 786440 | tf_op jit(solution)/shard_map/ppermute | solution.py:19
  201.2 1.3 copy-start.16
  202.5 0.9 copy-start.14
  460.9 5.1 %copy-start.10 = (f32[256,256]{1,0:T(8,128)S(1)}, f32[256,256]{1,0:T(8,128)}, u32[]{:S(2)}) copy-start(f32[256,256]{1,0:T(8,128)} %get-tuple-element.430) | copy-start | bytes 786436
Sparse Core Ops, SparseCore 0:
  202.6 258.2 all-reduce.2
where the time goes:
time: 477 us; the launch traced here: 474 us
  waiting for transfers between devices  178 us (37%)
  blocking collectives  79.5 us (17%)
  matrix products  75 us (16%)
  local copies, waits for them, and re-layouts  74.6 us (16%)
  other arithmetic  35.6 us (7%)
  starting transfers between devices  16.3 us (3%)
  between operations  14.7 us (3%)
    psum x1, waiting for transfers between devices, local(): lax.psum((grad_query, grad_key, grad_value, grad_out, grad_gain), ('dp',...  174 us
    psum x1, blocking collectives, local(): lax.psum((grad_query, grad_key, grad_value, grad_out, grad_gain), ('dp',...  79.5 us
    dot_general x16, matrix products, head_scores(): jnp.einsum('wbqe,wbke->wbqk', query_head, key_head, preferred_element_typ...  16.6 us
    ppermute x16, starting transfers between devices, swapped(): return lax.ppermute(block, axis, route)  16.2 us
    dot_general x8, matrix products, head_backward(): jnp.einsum('wbqk,wbqe->wbke', score_grad, query_head, preferred_element_t...  14.6 us
    unnamed x58, local copies, waits for them, and re-layouts  13 us
    dot_general x8, matrix products, head_forward(): jnp.einsum('wbqk,wbke->wbqe', weights, value_head, preferred_element_type...  10.7 us
  transfers between devices with their start and end apart: 17, of which 3 were waited for; matrix products, arithmetic and copies ran while one was open for 11% of the time, Pallas kernels for 0%

commit v1 on v0

v1 whole, which is shorter than its diff:
```python
import functools

import jax
import jax.numpy as jnp
from jax import lax
from jax.experimental import pallas as pl
from jax.experimental.pallas import tpu as pltpu
from jax.sharding import PartitionSpec as P

MESH = pl.DeviceIdType.MESH
HEADS = 8
SPAN = 256
WIDTH = 256
HEAD = 32
HALF = 128
GROUP_HEADS = 4
KEYS = 1280
CHUNKS = 5
ROUNDS = 4
ROWS = 512
NX = 8
NY = 8
ND = 4
EPS = 1e-06
LOG2E = 1.4426950408889634
SCALE = HEAD ** (-0.5)

f32 = jnp.float32
bf16 = jnp.bfloat16


def dot(a, b):
    return jnp.dot(a, b, preferred_element_type=f32)


def dot_nt(a, b):
    return lax.dot_general(a, b, (((1,), (1,)), ((), ())), preferred_element_type=f32)


def flipped(value, mask):
    out = value
    bit = 1
    while bit <= mask:
        if mask & bit:
            out = out + bit - 2 * bit * lax.rem(lax.div(value, bit), 2)
        bit *= 2
    return out


def fold(array, op):
    return op(array.reshape(array.shape[0] // 8, 8, array.shape[1]), axis=0)


def kernel(
    bits,
    x_ref, gain_ref, wq_ref, wk_ref, wv_ref, wo_ref, slot_ref, match_ref, cot_ref,
    upd_ref, ginp_ref, gq_ref, gk_ref, gv_ref, go_ref, gg_ref,
    oht, slot_f, inv_s, normed, nf0, nf1, nf2, nf3, normed_t,
    keys, vals, keys_t, vals_t, cots, qm, gm,
    att_t, dq_t, dkv, exps, ebuf, dsbuf, qpm, gpm,
    rd00, rd01, rd02, rd03, rd10, rd11, rd12, rd13,
    gf, gw, r1, s2, r2, s3, r3, a2, a1,
    ns_send, ns_recv, ds_send, ds_recv,
    s1_send, s1_recv, s2_send, s2_recv, s3_send, s3_recv,
    t2_send, t2_recv, t1_send, t1_recv,
):
    gi = lax.axis_index("graph")
    dp = lax.axis_index("dp")
    low = lax.rem(gi, NX)
    high = lax.div(gi, NX)
    far = (nf0, nf1, nf2, nf3)
    got = ((rd00, rd01, rd02, rd03), (rd10, rd11, rd12, rd13))
    partners = [flipped(gi, 1 << bit) for bit in bits]
    x_peer = [flipped(gi, d) for d in range(1, NX)]
    y_peer = [flipped(gi, d * NX) for d in range(1, NY)]
    d_peer = [flipped(dp, d) for d in range(1, ND)]

    barrier = pltpu.get_barrier_semaphore()
    for peer in x_peer + y_peer:
        pl.semaphore_signal(barrier, inc=1, device_id=(dp, peer), device_id_type=MESH)
    for peer in d_peer:
        pl.semaphore_signal(barrier, inc=1, device_id=(peer, gi), device_id_type=MESH)

    hot_t = (
        lax.broadcasted_iota(jnp.int32, (ROWS, ROWS), 0) == slot_ref[...] - gi * ROWS
    ).astype(f32).astype(bf16)
    oht[...] = hot_t
    hot = hot_t.T
    sx = dot(hot, x_ref[...])
    slot_f[...] = sx
    inv = lax.rsqrt(jnp.mean(sx * sx, axis=-1, keepdims=True) + EPS)
    inv_s[...] = inv
    gain = gain_ref[...]
    nrm = (sx * inv * gain).astype(bf16)
    for b in range(2):
        normed[b] = nrm[b * SPAN : (b + 1) * SPAN]

    pl.semaphore_wait(barrier, NX + NY + ND - 3)
    sends = []
    for r in range(ROUNDS):
        copy = pltpu.make_async_remote_copy(
            src_ref=normed, dst_ref=far[r], send_sem=ns_send.at[r], recv_sem=ns_recv.at[r],
            device_id=(dp, partners[r]), device_id_type=MESH,
        )
        copy.start()
        sends.append(copy)
    far_copies = list(sends)

    cs = dot(hot, cot_ref[...]).astype(bf16)
    cots[...] = cs
    wk_t = wk_ref[...].T
    wv_t = wv_ref[...].T
    q_t = dot_nt(wq_ref[...].T, nrm).astype(bf16)
    g_t = dot_nt(wo_ref[...], cs).astype(bf16)
    head_of = lax.broadcasted_iota(jnp.int32, (HALF, SPAN), 0) // HEAD
    for g in range(2):
        for b in range(2):
            qs = q_t[g * HALF : (g + 1) * HALF, b * SPAN : (b + 1) * SPAN]
            gs = g_t[g * HALF : (g + 1) * HALF, b * SPAN : (b + 1) * SPAN]
            for hh in range(GROUP_HEADS):
                qm[b, g, hh] = jnp.where(head_of == hh, qs, jnp.zeros_like(qs))
                gm[b, g, hh] = jnp.where(head_of == hh, gs, jnp.zeros_like(gs))

    def add_keys(b, c, rows):
        span = pl.ds(c * SPAN, SPAN)
        k = dot(rows, wk_ref[...]).astype(bf16)
        v = dot(rows, wv_ref[...]).astype(bf16)
        kt = dot_nt(wk_t, rows).astype(bf16)
        vt = dot_nt(wv_t, rows).astype(bf16)
        normed_t[b, :, span] = rows.T
        for g in range(2):
            half = slice(g * HALF, (g + 1) * HALF)
            keys[b, g, span, :] = k[:, half]
            vals[b, g, span, :] = v[:, half]
            keys_t[b, g, :, span] = kt[half]
            vals_t[b, g, :, span] = vt[half]

    pairs = [
        [lax.rem(match_ref[r, 2 * gi + b], 2) for b in range(2)] for r in range(ROUNDS)
    ]
    for b in range(2):
        add_keys(b, 0, normed[b])
    for r in range(ROUNDS):
        far_copies[r].wait_recv()
        for b in range(2):
            add_keys(b, r + 1, far[r][pairs[r][b]])

    def head(b, g, hh):
        slot = hh % 2
        lane = pl.ds(hh * SPAN, SPAN)
        row = pl.ds(hh * HEAD, HEAD)
        query = qm[b, g, hh]
        grad = gm[b, g, hh]
        top = None
        for c in range(CHUNKS):
            span = pl.ds(c * SPAN, SPAN)
            s = dot(keys[b, g, span, :], query)
            exps[slot, span, :] = s
            m = fold(s, jnp.max)
            top = m if top is None else jnp.maximum(top, m)
        top = jnp.max(top, axis=0, keepdims=True) * (SCALE * LOG2E)
        total = None
        o = None
        for c in range(CHUNKS):
            span = pl.ds(c * SPAN, SPAN)
            e = jnp.exp2(exps[slot, span, :] * (SCALE * LOG2E) - top)
            exps[slot, span, :] = e
            t = fold(e, jnp.sum)
            total = t if total is None else total + t
            eb = e.astype(bf16)
            ebuf[span, lane] = eb
            p = dot(vals_t[b, g, row, span], eb)
            o = p if o is None else o + p
        rinv = 1.0 / jnp.sum(total, axis=0, keepdims=True)
        o = o * rinv
        att_t[g, row, pl.ds(b * SPAN, SPAN)] = o.astype(bf16)
        mine = gm[b, g, hh, row, :].astype(f32)
        delta = jnp.sum(mine * o, axis=0, keepdims=True)
        qpm[:, lane] = (query.astype(f32) * (rinv * SCALE)).astype(bf16)
        gpm[:, lane] = (grad.astype(f32) * rinv).astype(bf16)
        dq = None
        for c in range(CHUNKS):
            span = pl.ds(c * SPAN, SPAN)
            dprob = dot(vals[b, g, span, :], grad)
            ds = (exps[slot, span, :] * (dprob - delta)).astype(bf16)
            dsbuf[span, lane] = ds
            p = dot(keys_t[b, g, row, span], ds)
            dq = p if dq is None else dq + p
        dq_t[g, row, pl.ds(b * SPAN, SPAN)] = (dq * (rinv * SCALE)).astype(bf16)

    def attend(b, g, hooks):
        for hh in range(GROUP_HEADS):
            head(b, g, hh)
            if hooks:
                hooks.pop(0)()
        for c in range(CHUNKS):
            span = pl.ds(c * SPAN, SPAN)
            dkv[g, c, 1, b] = dot_nt(ebuf[span, :], gpm[...]).astype(bf16)
            dkv[g, c, 0, b] = dot_nt(dsbuf[span, :], qpm[...]).astype(bf16)

    def weight_grads(g):
        gq = None
        gk = None
        gv = None
        for b in range(2):
            p = dot_nt(normed_t[b, :, 0:SPAN], dq_t[g, :, b * SPAN : (b + 1) * SPAN])
            gq = p if gq is None else gq + p
            for c in range(CHUNKS):
                nt = normed_t[b, :, c * SPAN : (c + 1) * SPAN]
                p = dot(nt, dkv[g, c, 0, b])
                gk = p if gk is None else gk + p
                p = dot(nt, dkv[g, c, 1, b])
                gv = p if gv is None else gv + p
        go = dot(att_t[g], cots[...])
        for at, part in (
            (0, gq), (256, gk), (512, gv), (768, go[:, :HALF]), (896, go[:, HALF:])
        ):
            n = part.shape[0]
            gf[g, at : at + n] = part
            gw[g, at : at + n] = part.astype(bf16)

    grads_far = [[], []]

    def send_grads(g):
        for r in range(ROUNDS):
            copy = pltpu.make_async_remote_copy(
                src_ref=dkv.at[g, r + 1], dst_ref=got[g][r],
                send_sem=ds_send.at[g, r], recv_sem=ds_recv.at[g, r],
                device_id=(dp, partners[r]), device_id_type=MESH,
            )
            copy.start()
            sends.append(copy)
            grads_far[g].append(copy)

    flight = {}

    def start(name, g, copies):
        for copy in copies:
            copy.start()
        sends.extend(copies)
        flight[name, g] = copies

    def arrived(name, g):
        for copy in flight[name, g]:
            copy.wait_recv()

    def remote(src, dst, send, recv, to):
        return pltpu.make_async_remote_copy(
            src_ref=src, dst_ref=dst, send_sem=send, recv_sem=recv,
            device_id=to, device_id_type=MESH,
        )

    def stage1(g):
        start("s1", g, [
            remote(
                gw.at[g, pl.ds(flipped(low, d) * 128, 128)], r1.at[g, d - 1],
                s1_send.at[g, d - 1], s1_recv.at[g, d - 1], (dp, x_peer[d - 1]),
            )
            for d in range(1, NX)
        ])

    def stage2(g):
        arrived("s1", g)
        total = gf[g, pl.ds(low * 128, 128)]
        for d in range(1, NX):
            total = total + r1[g, d - 1].astype(f32)
        s2[g] = total
        start("s2", g, [
            remote(
                s2.at[g, pl.ds(flipped(high, d) * 16, 16)], r2.at[g, d - 1],
                s2_send.at[g, d - 1], s2_recv.at[g, d - 1], (dp, y_peer[d - 1]),
            )
            for d in range(1, NY)
        ])

    def stage3(g):
        arrived("s2", g)
        total = s2[g, pl.ds(high * 16, 16)]
        for d in range(1, NY):
            total = total + r2[g, d - 1]
        s3[g] = total
        start("s3", g, [
            remote(
                s3.at[g], r3.at[g, d - 1],
                s3_send.at[g, d - 1], s3_recv.at[g, d - 1], (d_peer[d - 1], gi),
            )
            for d in range(1, ND)
        ])

    def stage4(g):
        arrived("s3", g)
        mine = pl.ds(high * 16, 16)
        a2[g, mine] = ((s3[g] + r3[g, 0]) + (r3[g, 1] + r3[g, 2])).astype(bf16)
        start("t2", g, [
            remote(
                a2.at[g, mine], a2.at[g, mine],
                t2_send.at[g, d - 1], t2_recv.at[g, d - 1], (dp, y_peer[d - 1]),
            )
            for d in range(1, NY)
        ])

    def stage5(g):
        arrived("t2", g)
        mine = pl.ds(low * 128, 128)
        start("t1", g, [
            remote(
                a2.at[g], a1.at[g, mine],
                t1_send.at[g, d - 1], t1_recv.at[g, d - 1], (dp, x_peer[d - 1]),
            )
            for d in range(1, NX)
        ])
        a1[g, mine] = a2[g]

    def finish(g):
        arrived("t1", g)
        cols = slice(g * HALF, (g + 1) * HALF)
        gq_ref[:, cols] = a1[g, 0:256].astype(f32)
        gk_ref[:, cols] = a1[g, 256:512].astype(f32)
        gv_ref[:, cols] = a1[g, 512:768].astype(f32)
        go_ref[cols, 0:HALF] = a1[g, 768:896].astype(f32)
        go_ref[cols, HALF:WIDTH] = a1[g, 896:1024].astype(f32)

    attend(0, 0, [])
    attend(1, 0, [])
    send_grads(0)
    weight_grads(0)
    stage1(0)
    none = lambda: None
    attend(0, 1, [none, lambda: stage2(0), none, lambda: stage3(0)])
    attend(1, 1, [none, lambda: stage4(0), lambda: stage5(0), lambda: finish(0)])
    weight_grads(1)
    stage1(1)
    send_grads(1)

    att = jnp.concatenate([att_t[0].T, att_t[1].T], axis=1)
    upd = dot(att, wo_ref[...]).astype(bf16)
    upd_ref[...] = dot(oht[...], upd).astype(bf16)
    stage2(1)
    qg = jnp.concatenate([dq_t[0].T, dq_t[1].T], axis=1)
    ng_q = dot_nt(qg, wq_ref[...])
    stage3(1)
    for copy in grads_far[0]:
        copy.wait_recv()
    stage4(1)
    for copy in grads_far[1]:
        copy.wait_recv()
    stage5(1)
    outs = []
    for b in range(2):
        sums = []
        for kv in range(2):
            halves = []
            for g in range(2):
                t = dkv[g, 0, kv, b].astype(f32)
                for r in range(ROUNDS):
                    t = t + got[g][r][kv, pairs[r][b]].astype(f32)
                halves.append(t.astype(bf16))
            sums.append(jnp.concatenate(halves, axis=1))
        rows = slice(b * SPAN, (b + 1) * SPAN)
        ng = ng_q[rows] + dot_nt(sums[0], wk_ref[...]) + dot_nt(sums[1], wv_ref[...])
        scaled = ng * gain
        x = slot_f[rows]
        iv = inv_s[rows]
        mean = jnp.mean(x * scaled, axis=-1, keepdims=True)
        outs.append((iv * scaled - x * (iv * iv * iv) * mean).astype(bf16))
    ginp_ref[...] = dot(oht[...], jnp.concatenate(outs, axis=0)).astype(bf16)
    finish(1)
    prod = (
        gq_ref[...] * wq_ref[...].astype(f32)
        + gk_ref[...] * wk_ref[...].astype(f32)
        + gv_ref[...] * wv_ref[...].astype(f32)
    )
    gg_ref[...] = jnp.sum(prod.T, axis=0, keepdims=True) / gain
    for copy in sends:
        copy.wait_send()


def local(inputs, gain, w_query, w_key, w_value, w_out, block_slots, matchings, cotangent):
    nbits = lax.axis_size("graph").bit_length() - 1
    rounds = matchings.shape[0]
    bits = tuple(turn * nbits // rounds for turn in range(rounds))
    vmem = pl.BlockSpec(memory_space=pltpu.VMEM)
    smem = pl.BlockSpec(memory_space=pltpu.SMEM)
    dma = pltpu.SemaphoreType.DMA
    far = pltpu.VMEM((2, SPAN, WIDTH), bf16)
    got = pltpu.VMEM((2, 2, SPAN, HALF), bf16)
    scratch = [
        pltpu.VMEM((ROWS, ROWS), bf16),
        pltpu.VMEM((ROWS, WIDTH), f32),
        pltpu.VMEM((ROWS, 1), f32),
        far, far, far, far, far,
        pltpu.VMEM((2, WIDTH, KEYS), bf16),
        pltpu.VMEM((2, 2, KEYS, HALF), bf16),
        pltpu.VMEM((2, 2, KEYS, HALF), bf16),
        pltpu.VMEM((2, 2, HALF, KEYS), bf16),
        pltpu.VMEM((2, 2, HALF, KEYS), bf16),
        pltpu.VMEM((ROWS, WIDTH), bf16),
        pltpu.VMEM((2, 2, GROUP_HEADS, HALF, SPAN), bf16),
        pltpu.VMEM((2, 2, GROUP_HEADS, HALF, SPAN), bf16),
        pltpu.VMEM((2, HALF, ROWS), bf16),
        pltpu.VMEM((2, HALF, ROWS), bf16),
        pltpu.VMEM((2, CHUNKS, 2, 2, SPAN, HALF), bf16),
        pltpu.VMEM((2, KEYS, SPAN), f32),
        pltpu.VMEM((KEYS, GROUP_HEADS * SPAN), bf16),
        pltpu.VMEM((KEYS, GROUP_HEADS * SPAN), bf16),
        pltpu.VMEM((HALF, GROUP_HEADS * SPAN), bf16),
        pltpu.VMEM((HALF, GROUP_HEADS * SPAN), bf16),
        got, got, got, got, got, got, got, got,
        pltpu.VMEM((2, 1024, HALF), f32),
        pltpu.VMEM((2, 1024, HALF), bf16),
        pltpu.VMEM((2, NX - 1, 128, HALF), bf16),
        pltpu.VMEM((2, 128, HALF), f32),
        pltpu.VMEM((2, NY - 1, 16, HALF), f32),
        pltpu.VMEM((2, 16, HALF), f32),
        pltpu.VMEM((2, ND - 1, 16, HALF), f32),
        pltpu.VMEM((2, 128, HALF), bf16),
        pltpu.VMEM((2, 1024, HALF), bf16),
        dma((ROUNDS,)), dma((ROUNDS,)), dma((2, ROUNDS)), dma((2, ROUNDS)),
        dma((2, NX - 1)), dma((2, NX - 1)), dma((2, NY - 1)), dma((2, NY - 1)),
        dma((2, ND - 1)), dma((2, ND - 1)),
        dma((2, NY - 1)), dma((2, NY - 1)), dma((2, NX - 1)), dma((2, NX - 1)),
    ]
    square = jax.ShapeDtypeStruct((WIDTH, WIDTH), f32)
    rows = jax.ShapeDtypeStruct((ROWS, WIDTH), bf16)
    update, grad_inputs, gq, gk, gv, go, gg = pl.pallas_call(
        functools.partial(kernel, bits),
        out_shape=(rows, rows, square, square, square, square,
                   jax.ShapeDtypeStruct((1, WIDTH), f32)),
        in_specs=[vmem] * 7 + [smem, vmem],
        out_specs=(vmem,) * 7,
        scratch_shapes=scratch,
        compiler_params=pltpu.CompilerParams(
            collective_id=0, has_side_effects=True, vmem_limit_bytes=56 * 2**20
        ),
    )(
        inputs[0], gain.reshape(1, WIDTH), w_query, w_key, w_value, w_out,
        block_slots.reshape(1, ROWS), matchings, cotangent[0],
    )
    return update[None], grad_inputs[None], gq, gk, gv, go, gg[0]


def solution(mesh):
    placed = (
        P("dp", "graph", None), P(), P(), P(), P(), P(), P("graph"), P(), P("dp", "graph", None),
    )
    return jax.shard_map(
        local,
        mesh=mesh,
        in_specs=placed,
        out_specs=(P("dp", "graph", None), P("dp", "graph", None), P(), P(), P(), P(), P()),
        check_vma=False,
    )
```

time: 477 us -> 94.8 us (0.20)
  waiting for transfers between devices: 178 us -> 0 us
  Pallas kernels: 0 us -> 86.7 us
  blocking collectives: 79.5 us -> 0 us
  matrix products: 75 us -> 0 us
  local copies, waits for them, and re-layouts: 74.6 us -> 7.16 us
  other arithmetic: 35.6 us -> 0 us
  starting transfers between devices: 16.3 us -> 0 us
  between operations: 14.7 us -> 0.66 us
    psum x1 -> x0, waiting for transfers between devices: 174 us -> none  [local(): lax.psum((grad_query, grad_key, grad_value, grad_out, grad_gain), ('dp',...]
    pallas_call x0 -> x1, Pallas kernels: none -> 86.7 us  [local(): pl.pallas_call(functools.partial(kernel, bits), out_shape=(rows, rows, sq...]
    psum x1 -> x0, blocking collectives: 79.5 us -> none  [local(): lax.psum((grad_query, grad_key, grad_value, grad_out, grad_gain), ('dp',...]
    dot_general x68 -> x0, matrix products: 75 us -> none  [the longest x16 16.6 us: head_scores(): jnp.einsum('wbqe,wbke->wbqk', query_head, key_head, preferred_element_typ...]
    gather x18 -> x0, local copies, waits for them, and re-layouts: 20.6 us -> none  [the longest x4 6.54 us: local(): far_keys.append(jnp.take(got_keys, pair_list[turn], axis=1))]
    ppermute x16 -> x0, starting transfers between devices: 16.2 us -> none  [swapped(): return lax.ppermute(block, axis, route)]
    convert_element_type x14 -> x0, other arithmetic: 9.95 us -> none  [the longest x4 5.13 us: local(): send_values.astype(jnp.bfloat16)]
    select_n x8 -> x0, local copies, waits for them, and re-layouts: 7.68 us -> none  [the longest x4 6.21 us: local(): far_values.append(jnp.take(got_values, pair_list[turn], axis=1))]
  transfers between devices with their start and end apart: 17 -> 0, of which waited for: 3 -> 0; matrix products, arithmetic and copies ran while one was open for 11% -> 0% of each run, Pallas kernels for 0% -> 0%
where the time goes in v1:
time: 94.8 us; the launch traced here: 94.6 us
  Pallas kernels  86.7 us (91%)
  local copies, waits for them, and re-layouts  7.16 us (8%)
    pallas_call x1, Pallas kernels, local(): pl.pallas_call(functools.partial(kernel, bits), out_shape=(rows, rows, sq...  86.7 us
    unnamed x19, local copies, waits for them, and re-layouts  7.16 us

profile of v1, /device:TPU:1, one launch (start us, length us, event | category | flops | bytes accessed | tf_op | source)
XLA Modules:
  0.0 94.6 jit_solution(5321867595639361871)
XLA Ops:
  0.6 86.7 %shard_map.144 = (bf16[512,256]{1,0:T(8,128)(2,1)}, bf16[512,256]{1,0:T(8,128)(2,1)}, f32[256,256]{1,0:T(8,128)}, f32[256,256]{1,0:T(8,128)}, f32[256,256]{1,0:T...) custom-call(bf16[512,256]{1,0:T(8,128)(2,1)} %bitcast.7, f32[1,256]{1,0:T(1,128)} %bitcast.12, bf16[256,256]{1,0:T(8,128)(2,1)} %wq_ref.1, ...), custom_call_target="tpu_custom_call" | custom-call | tf_op jit(solution)/shard_map/pallas_call | solution.py:425
  87.4 0.0 copy-start.4
  87.4 1.7 %copy.23 = bf16[1,512,256]{2,1,0:T(8,128)(2,1)} copy(bf16[1,512,256]{2,1,0:T(8,128)(2,1)} %bitcast.10) | data formatting | bytes 524288
  89.1 0.0 copy-done.4
  89.1 0.0 copy-start.3
  89.1 0.7 copy.24
  89.8 0.3 copy-done.3
  90.2 0.0 copy-start.2
  90.2 0.7 copy.25
  90.9 0.3 copy-done.2
  91.2 0.0 copy-start.1
  91.2 0.7 copy.26
  91.9 0.3 copy-done.1
  92.2 0.0 copy-start
  92.2 0.7 copy.27
  92.9 0.3 copy-done
  93.3 0.0 copy-start.5
  93.3 0.7 copy.28
  94.0 0.0 copy-done.5
  94.0 0.6 copy.29
Async XLA Ops:
  87.4 1.7 %copy-start.4 = (bf16[512,256]{1,0:T(8,128)(2,1)S(1)}, bf16[512,256]{1,0:T(8,128)(2,1)}, u32[]{:S(2)}) copy-start(bf16[512,256]{1,0:T(8,128)(2,1)} %get-tuple-element.15) | copy-start | bytes 786436
  89.1 1.0 %copy-start.3 = (f32[256,256]{1,0:T(8,128)S(1)}, f32[256,256]{1,0:T(8,128)}, u32[]{:S(2)}) copy-start(f32[256,256]{1,0:T(8,128)} %get-tuple-element.30) | copy-start | bytes 786436
  90.2 1.0 %copy-start.2 = (f32[256,256]{1,0:T(8,128)S(1)}, f32[256,256]{1,0:T(8,128)}, u32[]{:S(2)}) copy-start(f32[256,256]{1,0:T(8,128)} %get-tuple-element.31) | copy-start | bytes 786436
  91.2 1.0 %copy-start.1 = (f32[256,256]{1,0:T(8,128)S(1)}, f32[256,256]{1,0:T(8,128)}, u32[]{:S(2)}) copy-start(f32[256,256]{1,0:T(8,128)} %get-tuple-element.32) | copy-start | bytes 786436
  92.2 1.0 %copy-start = (f32[256,256]{1,0:T(8,128)S(1)}, f32[256,256]{1,0:T(8,128)}, u32[]{:S(2)}) copy-start(f32[256,256]{1,0:T(8,128)} %get-tuple-element.33) | copy-start | bytes 786436
  93.3 0.7 copy-start.5

commit v2 on v0

v2 whole, which is shorter than its diff:
```python
import functools

import jax
import jax.numpy as jnp
from jax import lax
from jax.experimental import pallas as pl
from jax.experimental.pallas import tpu as pltpu
from jax.sharding import PartitionSpec as P

MESH = pl.DeviceIdType.MESH
SPAN = 256
WIDTH = 256
HEAD = 32
HALF = 128
QUART = 64
PIECES = 4
KEYS = 1280
CHUNKS = 5
ROUNDS = 4
ROWS = 512
NX = 32
NZ = 8
EPS = 1e-06
LOG2E = 1.4426950408889634
SCALE = HEAD ** (-0.5)
GROUPS = ((0, 1), (2, 3))
EARLY = 2

f32 = jnp.float32
bf16 = jnp.bfloat16


def dot(a, b):
    return jnp.dot(a, b, preferred_element_type=f32)


def dot_nt(a, b):
    return lax.dot_general(a, b, (((1,), (1,)), ((), ())), preferred_element_type=f32)


def flipped(value, mask):
    out = value
    bit = 1
    while bit <= mask:
        if mask & bit:
            out = out + bit - 2 * bit * lax.rem(lax.div(value, bit), 2)
        bit *= 2
    return out


def fold(array, op):
    return op(array.reshape(array.shape[0] // 8, 8, array.shape[1]), axis=0)


def remote(src, dst, send, recv, to):
    return pltpu.make_async_remote_copy(
        src_ref=src, dst_ref=dst, send_sem=send, recv_sem=recv,
        device_id=to, device_id_type=MESH,
    )


def kernel(bits, *refs):
    (
        x_ref, gain_ref, wq_ref, wk_ref, wv_ref, wo_ref, slot_ref, match_ref, cot_ref,
        upd_ref, ginp_ref,
    ) = refs[:11]
    ng = len(GROUPS)
    a1 = refs[11 : 11 + ng]
    refs = refs[11 + ng :]
    (
        oht, slot_f, inv_s, normed, nf0, nf1, nf2, nf3, normed_t,
        keys, vals, keys_t, vals_t, cots_t, wkv, qm, gm,
        att_t, dq_t, dkv, exps, stack, mixer,
    ) = refs[:23]
    got = [refs[23 + 4 * p : 27 + 4 * p] for p in range(PIECES)]
    refs = refs[39:]
    gf, gw, r1, s2, r3 = [refs[ng * k : ng * k + ng] for k in range(5)]
    (
        ns_send, ns_recv, ds_send, ds_recv,
        s1_send, s1_recv, s3_send, s3_recv, t1_send, t1_recv,
    ) = refs[5 * ng :]

    gi = lax.axis_index("graph")
    dp = lax.axis_index("dp")
    spot = lax.rem(gi, 8) + 8 * lax.div(gi, 16)
    far = (nf0, nf1, nf2, nf3)
    partners = [(dp, flipped(gi, 1 << bit)) for bit in bits]
    x_peer = [(dp, flipped(gi, m % 8 + 16 * (m // 8))) for m in range(1, NX)]
    z_peer = [(flipped(dp, m // 2), flipped(gi, 8 * (m % 2))) for m in range(1, NZ)]

    barrier = pltpu.get_barrier_semaphore()
    for peer in x_peer + z_peer:
        pl.semaphore_signal(barrier, inc=1, device_id=peer, device_id_type=MESH)

    hot_t = (
        lax.broadcasted_iota(jnp.int32, (ROWS, ROWS), 0) == slot_ref[...] - gi * ROWS
    ).astype(f32).astype(bf16)
    oht[...] = hot_t
    hot = hot_t.T
    sx = dot(hot, x_ref[...])
    slot_f[...] = sx
    inv = lax.rsqrt(jnp.mean(sx * sx, axis=-1, keepdims=True) + EPS)
    inv_s[...] = inv
    gain = gain_ref[...]
    nrm = (sx * inv * gain).astype(bf16)
    for b in range(2):
        normed[b] = nrm[b * SPAN : (b + 1) * SPAN]

    pl.semaphore_wait(barrier, NX + NZ - 2)
    sends = []
    far_copies = []
    for r in range(ROUNDS):
        far_copies.append(
            remote(normed, far[r], ns_send.at[r], ns_recv.at[r], partners[r])
        )
    for copy in far_copies:
        copy.start()
        sends.append(copy)

    mixer[...] = jnp.zeros_like(mixer)
    cs = dot(hot, cot_ref[...]).astype(bf16)
    cots_t[...] = cs.T
    wk_t = wk_ref[...].T
    wv_t = wv_ref[...].T
    for p in range(PIECES):
        part = slice(p * QUART, (p + 1) * QUART)
        wkv[p * HALF : p * HALF + QUART] = wk_t[part]
        wkv[p * HALF + QUART : (p + 1) * HALF] = wv_t[part]
    q_t = dot_nt(wq_ref[...].T, nrm).astype(bf16)
    g_t = dot_nt(wo_ref[...], cs).astype(bf16)
    head_of = lax.broadcasted_iota(jnp.int32, (HALF, SPAN), 0) // HEAD
    for g in range(2):
        for b in range(2):
            qs = q_t[g * HALF : (g + 1) * HALF, b * SPAN : (b + 1) * SPAN]
            gs = g_t[g * HALF : (g + 1) * HALF, b * SPAN : (b + 1) * SPAN]
            for hh in range(4):
                qm[b, 4 * g + hh] = jnp.where(head_of == hh, qs, jnp.zeros_like(qs))
                gm[b, 4 * g + hh] = jnp.where(head_of == hh, gs, jnp.zeros_like(gs))

    def add_keys(b, c, rows):
        span = pl.ds(c * SPAN, SPAN)
        k = dot(rows, wk_ref[...]).astype(bf16)
        v = dot(rows, wv_ref[...]).astype(bf16)
        for g in range(2):
            half = slice(g * HALF, (g + 1) * HALF)
            keys[b, g, span, :] = k[:, half]
            vals[b, g, span, :] = v[:, half]
        keys_t[b, :, span] = dot_nt(wk_t, rows).astype(bf16)
        vals_t[b, :, span] = dot_nt(wv_t, rows).astype(bf16)
        normed_t[b, :, span] = rows.T

    units = [(p, b, 2 * p + i) for p in range(PIECES) for b in range(2) for i in range(2)]
    top = {}
    total = {}
    out = {}
    scale_of = {}
    shift = {}
    delta = {}
    dq = {}

    def scores(u, c):
        p, b, h = units[u]
        span = pl.ds(c * SPAN, SPAN)
        s = dot(keys[b, p // 2, span, :], qm[b, h])
        exps[u, span, :] = s
        m = fold(s, jnp.max)
        top[u] = m if c == 0 else jnp.maximum(top[u], m)

    def softmax(u, c):
        p, b, h = units[u]
        span = pl.ds(c * SPAN, SPAN)
        if c == 0:
            shift[u] = jnp.max(top[u], axis=0, keepdims=True) * (SCALE * LOG2E)
        e = jnp.exp2(exps[u, span, :] * (SCALE * LOG2E) - shift[u])
        exps[u, span, :] = e
        t = fold(e, jnp.sum)
        total[u] = t if c == 0 else total[u] + t
        eb = e.astype(bf16)
        stack[(u // 2) % 2, span, pl.ds((2 + u % 2) * SPAN, SPAN)] = eb
        o = dot(vals_t[b, pl.ds(h * HEAD, HEAD), span], eb)
        out[u] = o if c == 0 else out[u] + o

    def middle(u):
        p, b, h = units[u]
        i = u % 2
        rinv = 1.0 / jnp.sum(total[u], axis=0, keepdims=True)
        o = out[u] * rinv
        att_t[pl.ds(h * HEAD, HEAD), pl.ds(b * SPAN, SPAN)] = o.astype(bf16)
        row = pl.ds((h % 4) * HEAD, HEAD)
        grad = gm[b, h, row, :].astype(f32)
        query = qm[b, h, row, :].astype(f32)
        delta[u] = jnp.sum(grad * o, axis=0, keepdims=True)
        scale_of[u] = rinv * SCALE
        half = (u // 2) % 2
        mixer[half, pl.ds(i * HEAD, HEAD), pl.ds(i * SPAN, SPAN)] = (
            query * scale_of[u]
        ).astype(bf16)
        mixer[half, pl.ds(QUART + i * HEAD, HEAD), pl.ds((2 + i) * SPAN, SPAN)] = (
            grad * rinv
        ).astype(bf16)

    def score_grad(u, c):
        p, b, h = units[u]
        span = pl.ds(c * SPAN, SPAN)
        dprob = dot(vals[b, p // 2, span, :], gm[b, h])
        ds = (exps[u, span, :] * (dprob - delta[u])).astype(bf16)
        stack[(u // 2) % 2, span, pl.ds((u % 2) * SPAN, SPAN)] = ds
        q = dot(keys_t[b, pl.ds(h * HEAD, HEAD), span], ds)
        dq[u] = q if c == 0 else dq[u] + q

    def close(u):
        p, b, h = units[u]
        dq_t[pl.ds(h * HEAD, HEAD), pl.ds(b * SPAN, SPAN)] = (dq[u] * scale_of[u]).astype(bf16)

    def key_grads(u, c):
        p, b, h = units[u]
        half = (u // 2) % 2
        dkv[p, c, b] = dot_nt(
            stack[half, pl.ds(c * SPAN, SPAN), :], mixer[half]
        ).astype(bf16)

    def weight_grads(k):
        for i, p in enumerate(GROUPS[k]):
            feats = pl.ds(p * QUART, QUART)
            kv = None
            for b in range(2):
                for c in range(CHUNKS):
                    part = dot(normed_t[b, :, c * SPAN : (c + 1) * SPAN], dkv[p, c, b])
                    kv = part if kv is None else kv + part
            gq = dot_nt(normed_t[0, :, 0:SPAN], dq_t[feats, 0:SPAN]) + dot_nt(
                normed_t[1, :, 0:SPAN], dq_t[feats, SPAN:ROWS]
            )
            go = dot_nt(cots_t[...], att_t[feats, :])
            both = jnp.concatenate([gq, go], axis=1)
            at = i * ROWS
            gf[k][at : at + WIDTH] = kv
            gf[k][at + WIDTH : at + ROWS] = both
            gw[k][at : at + WIDTH] = kv.astype(bf16)
            gw[k][at + WIDTH : at + ROWS] = both.astype(bf16)

    grads_far = {}

    def send_grads(p):
        grads_far[p] = [
            remote(
                dkv.at[p, r + 1], got[p][r], ds_send.at[p, r], ds_recv.at[p, r], partners[r]
            )
            for r in range(ROUNDS)
        ]
        for copy in grads_far[p]:
            copy.start()
        sends.extend(grads_far[p])

    flight = {}

    def start(name, k, copies):
        for copy in copies:
            copy.start()
        sends.extend(copies)
        flight[name, k] = copies

    def arrived(name, k):
        for copy in flight[name, k]:
            copy.wait_recv()

    def spread(k):
        n = len(GROUPS[k]) * ROWS // NX
        start("s1", k, [
            remote(
                gw[k].at[pl.ds(flipped(spot, m) * n, n)], r1[k].at[m - 1],
                s1_send.at[k, m - 1], s1_recv.at[k, m - 1], x_peer[m - 1],
            )
            for m in range(1, NX)
        ])

    def across(k):
        n = len(GROUPS[k]) * ROWS // NX
        arrived("s1", k)
        acc = gf[k][pl.ds(spot * n, n)]
        for m in range(1, NX):
            acc = acc + r1[k][m - 1].astype(f32)
        s2[k][...] = acc
        start("s3", k, [
            remote(
                s2[k], r3[k].at[m - 1],
                s3_send.at[k, m - 1], s3_recv.at[k, m - 1], z_peer[m - 1],
            )
            for m in range(1, NZ)
        ])

    def gather(k):
        n = len(GROUPS[k]) * ROWS // NX
        arrived("s3", k)
        mine = pl.ds(spot * n, n)
        level = [s2[k][...]] + [r3[k][m - 1] for m in range(1, NZ)]
        while len(level) > 1:
            level = [level[j] + level[j + 1] for j in range(0, len(level), 2)]
        a1[k][mine] = level[0].astype(bf16)
        start("t1", k, [
            remote(
                a1[k].at[mine], a1[k].at[mine],
                t1_send.at[k, m - 1], t1_recv.at[k, m - 1], x_peer[m - 1],
            )
            for m in range(1, NX)
        ])

    for b in range(2):
        add_keys(b, 0, normed[b])
    for u in range(len(units)):
        for c in range(min(EARLY, 1)):
            scores(u, c)
    pairs = [
        [lax.rem(match_ref[r, 2 * gi + b], 2) for b in range(2)] for r in range(ROUNDS)
    ]
    for r in range(ROUNDS):
        far_copies[r].wait_recv()
        for b in range(2):
            add_keys(b, r + 1, far[r][pairs[r][b]])
        if r + 1 < EARLY:
            for u in range(len(units)):
                scores(u, r + 1)

    hooks = {
        4: [lambda: send_grads(0)],
        8: [lambda: send_grads(1), lambda: weight_grads(0), lambda: spread(0)],
        12: [lambda: send_grads(2), lambda: across(0)],
        15: [lambda: gather(0)],
    }
    last = len(units) - 1
    for c in range(EARLY, CHUNKS):
        scores(0, c)
    for u in range(len(units)):
        for c in range(CHUNKS):
            if u < last and c >= EARLY:
                scores(u + 1, c)
            softmax(u, c)
        middle(u)
        for c in range(CHUNKS):
            score_grad(u, c)
            if u % 2 == 0 and u >= 2:
                key_grads(u - 1, c)
        close(u)
        for hook in hooks.get(u, []):
            hook()
    for c in range(CHUNKS):
        key_grads(last, c)
    weight_grads(1)
    spread(1)
    send_grads(3)

    upd = dot(att_t[...].T, wo_ref[...]).astype(bf16)
    upd_ref[...] = dot(oht[...], upd).astype(bf16)
    ng_q = dot_nt(dq_t[...].T, wq_ref[...])
    across(1)

    def key_total(p, b):
        t = dkv[p, 0, b].astype(f32)
        for r in range(ROUNDS):
            t = t + got[p][r][pairs[r][b]].astype(f32)
        return t.astype(bf16)

    for p in range(PIECES):
        for copy in grads_far[p]:
            copy.wait_recv()
    outs = []
    for b in range(2):
        sums = jnp.concatenate([key_total(p, b) for p in range(PIECES)], axis=1)
        rows = slice(b * SPAN, (b + 1) * SPAN)
        ngrad = ng_q[rows] + dot(sums, wkv[...])
        scaled = ngrad * gain
        x = slot_f[rows]
        iv = inv_s[rows]
        mean = jnp.mean(x * scaled, axis=-1, keepdims=True)
        outs.append((iv * scaled - x * (iv * iv * iv) * mean).astype(bf16))
    ginp_ref[...] = dot(oht[...], jnp.concatenate(outs, axis=0)).astype(bf16)
    gather(1)
    for k in range(ng):
        arrived("t1", k)
    for copy in sends:
        copy.wait_send()


def finish(*refs):
    ng = len(GROUPS)
    upd, ginp = refs[:2]
    sums = refs[2 : 2 + ng]
    gain_ref, wq_ref, wk_ref, wv_ref = refs[2 + ng : 6 + ng]
    upd_ref, ginp_ref, gq_ref, gk_ref, gv_ref, go_ref, gg_ref = refs[6 + ng :]
    upd_ref[...] = upd[...]
    ginp_ref[...] = ginp[...]
    kv = {}
    qo = {}
    for k, group in enumerate(GROUPS):
        for i, p in enumerate(group):
            at = i * ROWS
            kv[p] = sums[k][at : at + WIDTH].astype(f32)
            qo[p] = sums[k][at + WIDTH : at + ROWS].astype(f32)
    first, second = slice(0, QUART), slice(QUART, HALF)

    def joined(parts, half):
        return jnp.concatenate([parts[p][:, half] for p in range(PIECES)], axis=1)

    gk, gv, gq = joined(kv, first), joined(kv, second), joined(qo, first)
    gq_ref[...] = gq
    gk_ref[...] = gk
    gv_ref[...] = gv
    go_ref[...] = joined(qo, second).T
    prod = (
        gq * wq_ref[...].astype(f32) + gk * wk_ref[...].astype(f32)
        + gv * wv_ref[...].astype(f32)
    )
    gg_ref[...] = jnp.sum(prod.T, axis=0, keepdims=True) / gain_ref[...]


def local(inputs, gain, w_query, w_key, w_value, w_out, block_slots, matchings, cotangent):
    nbits = lax.axis_size("graph").bit_length() - 1
    rounds = matchings.shape[0]
    bits = tuple(turn * nbits // rounds for turn in range(rounds))
    vmem = pl.BlockSpec(memory_space=pltpu.VMEM)
    smem = pl.BlockSpec(memory_space=pltpu.SMEM)
    dma = pltpu.SemaphoreType.DMA
    ng = len(GROUPS)
    size = [len(group) * ROWS for group in GROUPS]
    far = pltpu.VMEM((2, SPAN, WIDTH), bf16)
    got = pltpu.VMEM((2, SPAN, HALF), bf16)
    units = 4 * PIECES
    scratch = [
        pltpu.VMEM((ROWS, ROWS), bf16),
        pltpu.VMEM((ROWS, WIDTH), f32),
        pltpu.VMEM((ROWS, 1), f32),
        far, far, far, far, far,
        pltpu.VMEM((2, WIDTH, KEYS), bf16),
        pltpu.VMEM((2, 2, KEYS, HALF), bf16),
        pltpu.VMEM((2, 2, KEYS, HALF), bf16),
        pltpu.VMEM((2, WIDTH, KEYS), bf16),
        pltpu.VMEM((2, WIDTH, KEYS), bf16),
        pltpu.VMEM((WIDTH, ROWS), bf16),
        pltpu.VMEM((ROWS, WIDTH), bf16),
        pltpu.VMEM((2, 8, HALF, SPAN), bf16),
        pltpu.VMEM((2, 8, HALF, SPAN), bf16),
        pltpu.VMEM((WIDTH, ROWS), bf16),
        pltpu.VMEM((WIDTH, ROWS), bf16),
        pltpu.VMEM((PIECES, CHUNKS, 2, SPAN, HALF), bf16),
        pltpu.VMEM((units, KEYS, SPAN), f32),
        pltpu.VMEM((2, KEYS, 4 * SPAN), bf16),
        pltpu.VMEM((2, HALF, 4 * SPAN), bf16),
    ]
    scratch += [got] * (PIECES * ROUNDS)
    scratch += [pltpu.VMEM((n, HALF), f32) for n in size]
    scratch += [pltpu.VMEM((n, HALF), bf16) for n in size]
    scratch += [pltpu.VMEM((NX - 1, n // NX, HALF), bf16) for n in size]
    scratch += [pltpu.VMEM((n // NX, HALF), f32) for n in size]
    scratch += [pltpu.VMEM((NZ - 1, n // NX, HALF), f32) for n in size]
    scratch += [
        dma((ROUNDS,)), dma((ROUNDS,)), dma((PIECES, ROUNDS)), dma((PIECES, ROUNDS)),
        dma((ng, NX - 1)), dma((ng, NX - 1)), dma((ng, NZ - 1)), dma((ng, NZ - 1)),
        dma((ng, NX - 1)), dma((ng, NX - 1)),
    ]
    square = jax.ShapeDtypeStruct((WIDTH, WIDTH), f32)
    rows = jax.ShapeDtypeStruct((ROWS, WIDTH), bf16)
    gain_row = gain.reshape(1, WIDTH)
    parts = pl.pallas_call(
        functools.partial(kernel, bits),
        out_shape=(rows, rows) + tuple(jax.ShapeDtypeStruct((n, HALF), bf16) for n in size),
        in_specs=[vmem] * 7 + [smem, vmem],
        out_specs=(vmem,) * (2 + ng),
        scratch_shapes=scratch,
        compiler_params=pltpu.CompilerParams(
            collective_id=0, has_side_effects=True, vmem_limit_bytes=58 * 2**20
        ),
    )(
        inputs[0], gain_row, w_query, w_key, w_value, w_out,
        block_slots.reshape(1, ROWS), matchings, cotangent[0],
    )
    update, grad_inputs, gq, gk, gv, go, gg = pl.pallas_call(
        finish,
        out_shape=(rows, rows, square, square, square, square,
                   jax.ShapeDtypeStruct((1, WIDTH), f32)),
        in_specs=[vmem] * (6 + ng),
        out_specs=(vmem,) * 7,
    )(*parts, gain_row, w_query, w_key, w_value)
    return update[None], grad_inputs[None], gq, gk, gv, go, gg[0]


def solution(mesh):
    placed = (
        P("dp", "graph", None), P(), P(), P(), P(), P(), P("graph"), P(), P("dp", "graph", None),
    )
    return jax.shard_map(
        local,
        mesh=mesh,
        in_specs=placed,
        out_specs=(P("dp", "graph", None), P("dp", "graph", None), P(), P(), P(), P(), P()),
        check_vma=False,
    )
```

time: 477 us -> 74.7 us (0.16)
  waiting for transfers between devices: 178 us -> 0 us
  blocking collectives: 79.5 us -> 0 us
  matrix products: 75 us -> 0 us
  local copies, waits for them, and re-layouts: 74.6 us -> 0 us
  Pallas kernels: 0 us -> 73.9 us
  other arithmetic: 35.6 us -> 0 us
  starting transfers between devices: 16.3 us -> 0 us
  between operations: 14.7 us -> 0.64 us
    psum x1 -> x0, waiting for transfers between devices: 174 us -> none  [local(): lax.psum((grad_query, grad_key, grad_value, grad_out, grad_gain), ('dp',...]
    psum x1 -> x0, blocking collectives: 79.5 us -> none  [local(): lax.psum((grad_query, grad_key, grad_value, grad_out, grad_gain), ('dp',...]
    dot_general x68 -> x0, matrix products: 75 us -> none  [the longest x16 16.6 us: head_scores(): jnp.einsum('wbqe,wbke->wbqk', query_head, key_head, preferred_element_typ...]
    pallas_call x0 -> x2, Pallas kernels: none -> 73.9 us  [the longest x1 71.2 us: local(): pl.pallas_call(functools.partial(kernel, bits), out_shape=(rows, rows) +...]
    gather x18 -> x0, local copies, waits for them, and re-layouts: 20.6 us -> none  [the longest x4 6.54 us: local(): far_keys.append(jnp.take(got_keys, pair_list[turn], axis=1))]
    ppermute x16 -> x0, starting transfers between devices: 16.2 us -> none  [swapped(): return lax.ppermute(block, axis, route)]
    unnamed x58 -> x0, local copies, waits for them, and re-layouts: 13 us -> none
    convert_element_type x14 -> x0, other arithmetic: 9.95 us -> none  [the longest x4 5.13 us: local(): send_values.astype(jnp.bfloat16)]
  transfers between devices with their start and end apart: 17 -> 0, of which waited for: 3 -> 0; matrix products, arithmetic and copies ran while one was open for 11% -> 0% of each run, Pallas kernels for 0% -> 0%
where the time goes in v2:
time: 74.7 us; the launch traced here: 74.6 us
  Pallas kernels  73.9 us (99%)
    pallas_call x1, Pallas kernels, local(): pl.pallas_call(functools.partial(kernel, bits), out_shape=(rows, rows) +...  71.2 us
    pallas_call x1, Pallas kernels, local(): pl.pallas_call(finish, out_shape=(rows, rows, square, square, square, squ...  2.73 us

profile of v2, /device:TPU:1, one launch (start us, length us, event | category | flops | bytes accessed | tf_op | source)
XLA Modules:
  0.0 74.6 jit_solution(12334978934850333724)
XLA Ops:
  0.6 71.2 %shard_map.144 = (bf16[512,256]{1,0:T(8,128)(2,1)}, bf16[512,256]{1,0:T(8,128)(2,1)}, bf16[1024,128]{1,0:T(8,128)(2,1)}, bf16[1024,128]{1,0:T(8,128)(2,1)}) custom-call(bf16[512,256]{1,0:T(8,128)(2,1)} %bitcast.7, f32[1,256]{1,0:T(1,128)} %bitcast.9, bf16[256,256]{1,0:T(8,128)(2,1)} %refs_5_.3, bf16[256,256]{1,0:T(8,128)(2,1)} %refs_6_.1, ...), custom_call_target="tpu_custom_call" | custom-call | tf_op jit(solution)/shard_map/pallas_call | solution.py:462
  71.8 2.7 %shard_map.145 = (bf16[512,256]{1,0:T(8,128)(2,1)}, bf16[512,256]{1,0:T(8,128)(2,1)}, f32[256,256]{1,0:T(8,128)}, f32[256,256]{1,0:T(8,128)}, f32[256,256]{1,0:T...) custom-call(bf16[512,256]{1,0:T(8,128)(2,1)} %get-tuple-element.18.refs_0_, bf16[512,256]{1,0:T(8,128)(2,1)} %get-tuple-element.19.refs_1_, ...), custom_call_target="tpu_custom_call" | custom-call | tf_op jit(solution)/shard_map/pallas_call | solution.py:475

commit v3 on v2

--- a/solution.py
+++ b/solution.py
@@ -23,7 +23,7 @@
 EPS = 1e-06
 LOG2E = 1.4426950408889634
 SCALE = HEAD ** (-0.5)
-GROUPS = ((0, 1), (2, 3))
+GROUPS = ((0, 1, 2), (3,))
 EARLY = 2
 
 f32 = jnp.float32
@@ -77,7 +77,7 @@
     gf, gw, r1, s2, r3 = [refs[ng * k : ng * k + ng] for k in range(5)]
     (
         ns_send, ns_recv, ds_send, ds_recv,
-        s1_send, s1_recv, s3_send, s3_recv, t1_send, t1_recv,
+        s1_send, s1_recv, s3_send, s3_recv, t1_send, t1_recv, news_x, news_z,
     ) = refs[5 * ng :]
 
     gi = lax.axis_index("graph")
@@ -89,8 +89,19 @@
     z_peer = [(flipped(dp, m // 2), flipped(gi, 8 * (m % 2))) for m in range(1, NZ)]
 
     barrier = pltpu.get_barrier_semaphore()
-    for peer in x_peer + z_peer:
+    x_step = [x_peer[m - 1] for m in (1, 2, 4, 8, 16)]
+    z_step = [z_peer[m - 1] for m in (1, 2, 6)]
+    for peer in x_step + z_step:
         pl.semaphore_signal(barrier, inc=1, device_id=peer, device_id_type=MESH)
+
+    def tell(k):
+        for step, news in ((x_step, news_x), (z_step, news_z)):
+            if 1 <= k <= len(step):
+                pl.semaphore_wait(news.at[k - 1], 1)
+            if k < len(step):
+                pl.semaphore_signal(
+                    news.at[k], inc=1, device_id=step[k], device_id_type=MESH
+                )
 
     hot_t = (
         lax.broadcasted_iota(jnp.int32, (ROWS, ROWS), 0) == slot_ref[...] - gi * ROWS
@@ -106,7 +117,7 @@
     for b in range(2):
         normed[b] = nrm[b * SPAN : (b + 1) * SPAN]
 
-    pl.semaphore_wait(barrier, NX + NZ - 2)
+    pl.semaphore_wait(barrier, 8)
     sends = []
     far_copies = []
     for r in range(ROUNDS):
@@ -116,6 +127,7 @@
     for copy in far_copies:
         copy.start()
         sends.append(copy)
+    tell(0)
 
     mixer[...] = jnp.zeros_like(mixer)
     cs = dot(hot, cot_ref[...]).astype(bf16)
@@ -304,6 +316,7 @@
             for m in range(1, NX)
         ])
 
+    tell(1)
     for b in range(2):
         add_keys(b, 0, normed[b])
     for u in range(len(units)):
@@ -313,6 +326,8 @@
         [lax.rem(match_ref[r, 2 * gi + b], 2) for b in range(2)] for r in range(ROUNDS)
     ]
     for r in range(ROUNDS):
+        if r == 1:
+            tell(2)
         far_copies[r].wait_recv()
         for b in range(2):
             add_keys(b, r + 1, far[r][pairs[r][b]])
@@ -320,11 +335,12 @@
             for u in range(len(units)):
                 scores(u, r + 1)
 
+    tell(3)
     hooks = {
-        4: [lambda: send_grads(0)],
-        8: [lambda: send_grads(1), lambda: weight_grads(0), lambda: spread(0)],
-        12: [lambda: send_grads(2), lambda: across(0)],
-        15: [lambda: gather(0)],
+        2: [lambda: tell(4)],
+        4: [lambda: tell(5), lambda: send_grads(0)],
+        8: [lambda: send_grads(1)],
+        12: [lambda: weight_grads(0), lambda: spread(0), lambda: send_grads(2)],
     }
     last = len(units) - 1
     for c in range(EARLY, CHUNKS):
@@ -350,15 +366,15 @@
 
     upd = dot(att_t[...].T, wo_ref[...]).astype(bf16)
     upd_ref[...] = dot(oht[...], upd).astype(bf16)
+    across(0)
     ng_q = dot_nt(dq_t[...].T, wq_ref[...])
-    across(1)
-
     def key_total(p, b):
         t = dkv[p, 0, b].astype(f32)
         for r in range(ROUNDS):
             t = t + got[p][r][pairs[r][b]].astype(f32)
         return t.astype(bf16)
 
+    across(1)
     for p in range(PIECES):
         for copy in grads_far[p]:
             copy.wait_recv()
@@ -373,6 +389,7 @@
         mean = jnp.mean(x * scaled, axis=-1, keepdims=True)
         outs.append((iv * scaled - x * (iv * iv * iv) * mean).astype(bf16))
     ginp_ref[...] = dot(oht[...], jnp.concatenate(outs, axis=0)).astype(bf16)
+    gather(0)
     gather(1)
     for k in range(ng):
         arrived("t1", k)
@@ -455,6 +472,7 @@
         dma((ROUNDS,)), dma((ROUNDS,)), dma((PIECES, ROUNDS)), dma((PIECES, ROUNDS)),
         dma((ng, NX - 1)), dma((ng, NX - 1)), dma((ng, NZ - 1)), dma((ng, NZ - 1)),
         dma((ng, NX - 1)), dma((ng, NX - 1)),
+        pltpu.SemaphoreType.REGULAR((5,)), pltpu.SemaphoreType.REGULAR((3,)),
     ]
     square = jax.ShapeDtypeStruct((WIDTH, WIDTH), f32)
     rows = jax.ShapeDtypeStruct((ROWS, WIDTH), bf16)

time: 74.7 us -> 68.3 us (0.914)
  Pallas kernels: 73.9 us -> 67.5 us
    pallas_call x1, Pallas kernels: 71.2 us -> 64.7 us  [local(): pl.pallas_call(functools.partial(kernel, bits), out_shape=(rows, rows) +...]
where the time goes in v3:
time: 68.3 us; the launch traced here: 68.1 us
  Pallas kernels  67.5 us (99%)
    pallas_call x1, Pallas kernels, local(): pl.pallas_call(functools.partial(kernel, bits), out_shape=(rows, rows) +...  64.7 us
    pallas_call x1, Pallas kernels, local(): pl.pallas_call(finish, out_shape=(rows, rows, square, square, square, squ...  2.78 us

profile of v3, /device:TPU:1, one launch (start us, length us, event | category | flops | bytes accessed | tf_op | source)
XLA Modules:
  0.0 68.1 jit_solution(11927570441483878827)
XLA Ops:
  0.6 64.7 %shard_map.144 = (bf16[512,256]{1,0:T(8,128)(2,1)}, bf16[512,256]{1,0:T(8,128)(2,1)}, bf16[1536,128]{1,0:T(8,128)(2,1)}, bf16[512,128]{1,0:T(8,128)(2,1)}) custom-call(bf16[512,256]{1,0:T(8,128)(2,1)} %bitcast.7, f32[1,256]{1,0:T(1,128)} %bitcast.9, bf16[256,256]{1,0:T(8,128)(2,1)} %refs_5_.3, bf16[256,256]{1,0:T(8,128)(2,1)} %refs_6_.1, ...), custom_call_target="tpu_custom_call" | custom-call | tf_op jit(solution)/shard_map/pallas_call | solution.py:480
  65.3 2.8 %shard_map.145 = (bf16[512,256]{1,0:T(8,128)(2,1)}, bf16[512,256]{1,0:T(8,128)(2,1)}, f32[256,256]{1,0:T(8,128)}, f32[256,256]{1,0:T(8,128)}, f32[256,256]{1,0:T...) custom-call(bf16[512,256]{1,0:T(8,128)(2,1)} %get-tuple-element.18.refs_0_, bf16[512,256]{1,0:T(8,128)(2,1)} %get-tuple-element.19.refs_1_, ...), custom_call_target="tpu_custom_call" | custom-call | tf_op jit(solution)/shard_map/pallas_call | solution.py:493

commit v4 on v3

--- a/solution.py
+++ b/solution.py
@@ -25,6 +25,9 @@
 SCALE = HEAD ** (-0.5)
 GROUPS = ((0, 1, 2), (3,))
 EARLY = 2
+RING4 = (0, 1, 2, 1)
+X_ORDER = sorted(range(1, NX), key=lambda m: -RING4[m // 2 % 4] - RING4[m // 8])
+Z_ORDER = sorted(range(1, NZ), key=lambda m: -2 * RING4[m // 2] - m % 2)
 
 f32 = jnp.float32
 bf16 = jnp.bfloat16
@@ -282,7 +285,7 @@
                 gw[k].at[pl.ds(flipped(spot, m) * n, n)], r1[k].at[m - 1],
                 s1_send.at[k, m - 1], s1_recv.at[k, m - 1], x_peer[m - 1],
             )
-            for m in range(1, NX)
+            for m in X_ORDER
         ])
 
     def across(k):
@@ -297,7 +300,7 @@
                 s2[k], r3[k].at[m - 1],
                 s3_send.at[k, m - 1], s3_recv.at[k, m - 1], z_peer[m - 1],
             )
-            for m in range(1, NZ)
+            for m in Z_ORDER
         ])
 
     def gather(k):
@@ -313,7 +316,7 @@
                 a1[k].at[mine], a1[k].at[mine],
                 t1_send.at[k, m - 1], t1_recv.at[k, m - 1], x_peer[m - 1],
             )
-            for m in range(1, NX)
+            for m in X_ORDER
         ])
 
     tell(1)
@@ -375,6 +378,7 @@
         return t.astype(bf16)
 
     across(1)
+    gather(0)
     for p in range(PIECES):
         for copy in grads_far[p]:
             copy.wait_recv()
@@ -389,7 +393,6 @@
         mean = jnp.mean(x * scaled, axis=-1, keepdims=True)
         outs.append((iv * scaled - x * (iv * iv * iv) * mean).astype(bf16))
     ginp_ref[...] = dot(oht[...], jnp.concatenate(outs, axis=0)).astype(bf16)
-    gather(0)
     gather(1)
     for k in range(ng):
         arrived("t1", k)

time: 68.3 us -> 66.2 us (0.969)
  Pallas kernels: 67.5 us -> 65.4 us
    pallas_call x1, Pallas kernels: 64.7 us -> 62.7 us  [local(): pl.pallas_call(functools.partial(kernel, bits), out_shape=(rows, rows) +...]
where the time goes in v4:
time: 66.2 us; the launch traced here: 66.1 us
  Pallas kernels  65.4 us (99%)
    pallas_call x1, Pallas kernels, local(): pl.pallas_call(functools.partial(kernel, bits), out_shape=(rows, rows) +...  62.7 us
    pallas_call x1, Pallas kernels, local(): pl.pallas_call(finish, out_shape=(rows, rows, square, square, square, squ...  2.78 us

profile of v4, /device:TPU:1, one launch (start us, length us, event | category | flops | bytes accessed | tf_op | source)
XLA Modules:
  0.0 66.1 jit_solution(4772554466254673824)
XLA Ops:
  0.6 62.7 %shard_map.144 = (bf16[512,256]{1,0:T(8,128)(2,1)}, bf16[512,256]{1,0:T(8,128)(2,1)}, bf16[1536,128]{1,0:T(8,128)(2,1)}, bf16[512,128]{1,0:T(8,128)(2,1)}) custom-call(bf16[512,256]{1,0:T(8,128)(2,1)} %bitcast.7, f32[1,256]{1,0:T(1,128)} %bitcast.9, bf16[256,256]{1,0:T(8,128)(2,1)} %refs_5_.3, bf16[256,256]{1,0:T(8,128)(2,1)} %refs_6_.1, ...), custom_call_target="tpu_custom_call" | custom-call | tf_op jit(solution)/shard_map/pallas_call | solution.py:483
  63.3 2.8 %shard_map.145 = (bf16[512,256]{1,0:T(8,128)(2,1)}, bf16[512,256]{1,0:T(8,128)(2,1)}, f32[256,256]{1,0:T(8,128)}, f32[256,256]{1,0:T(8,128)}, f32[256,256]{1,0:T...) custom-call(bf16[512,256]{1,0:T(8,128)(2,1)} %get-tuple-element.18.refs_0_, bf16[512,256]{1,0:T(8,128)(2,1)} %get-tuple-element.19.refs_1_, ...), custom_call_target="tpu_custom_call" | custom-call | tf_op jit(solution)/shard_map/pallas_call | solution.py:496

commit v5 on v4

--- a/solution.py
+++ b/solution.py
@@ -64,7 +64,7 @@
 
 def kernel(bits, *refs):
     (
-        x_ref, gain_ref, wq_ref, wk_ref, wv_ref, wo_ref, slot_ref, match_ref, cot_ref,
+        x_hbm, gain_ref, wq_hbm, wk_hbm, wv_hbm, wo_hbm, slot_ref, match_ref, cot_hbm,
         upd_ref, ginp_ref,
     ) = refs[:11]
     ng = len(GROUPS)
@@ -81,6 +81,7 @@
     (
         ns_send, ns_recv, ds_send, ds_recv,
         s1_send, s1_recv, s3_send, s3_recv, t1_send, t1_recv, news_x, news_z,
+        x_ref, cot_ref, wq_ref, wk_ref, wv_ref, wo_ref, in_sem,
     ) = refs[5 * ng :]
 
     gi = lax.axis_index("graph")
@@ -106,11 +107,22 @@
                     news.at[k], inc=1, device_id=step[k], device_id_type=MESH
                 )
 
+    loads = [
+        pltpu.make_async_copy(src, dst, in_sem.at[j])
+        for j, (src, dst) in enumerate((
+            (x_hbm, x_ref), (cot_hbm, cot_ref), (wk_hbm, wk_ref), (wv_hbm, wv_ref),
+            (wq_hbm, wq_ref), (wo_hbm, wo_ref),
+        ))
+    ]
+    for load in loads:
+        load.start()
+
     hot_t = (
         lax.broadcasted_iota(jnp.int32, (ROWS, ROWS), 0) == slot_ref[...] - gi * ROWS
     ).astype(f32).astype(bf16)
     oht[...] = hot_t
     hot = hot_t.T
+    loads[0].wait()
     sx = dot(hot, x_ref[...])
     slot_f[...] = sx
     inv = lax.rsqrt(jnp.mean(sx * sx, axis=-1, keepdims=True) + EPS)
@@ -133,6 +145,8 @@
     tell(0)
 
     mixer[...] = jnp.zeros_like(mixer)
+    for load in loads[1:]:
+        load.wait()
     cs = dot(hot, cot_ref[...]).astype(bf16)
     cots_t[...] = cs.T
     wk_t = wk_ref[...].T
@@ -438,6 +452,7 @@
     bits = tuple(turn * nbits // rounds for turn in range(rounds))
     vmem = pl.BlockSpec(memory_space=pltpu.VMEM)
     smem = pl.BlockSpec(memory_space=pltpu.SMEM)
+    whole = pl.BlockSpec(memory_space=pl.ANY)
     dma = pltpu.SemaphoreType.DMA
     ng = len(GROUPS)
     size = [len(group) * ROWS for group in GROUPS]
@@ -476,6 +491,10 @@
         dma((ng, NX - 1)), dma((ng, NX - 1)), dma((ng, NZ - 1)), dma((ng, NZ - 1)),
         dma((ng, NX - 1)), dma((ng, NX - 1)),
         pltpu.SemaphoreType.REGULAR((5,)), pltpu.SemaphoreType.REGULAR((3,)),
+        pltpu.VMEM((ROWS, WIDTH), bf16), pltpu.VMEM((ROWS, WIDTH), bf16),
+        pltpu.VMEM((WIDTH, WIDTH), bf16), pltpu.VMEM((WIDTH, WIDTH), bf16),
+        pltpu.VMEM((WIDTH, WIDTH), bf16), pltpu.VMEM((WIDTH, WIDTH), bf16),
+        dma((6,)),
     ]
     square = jax.ShapeDtypeStruct((WIDTH, WIDTH), f32)
     rows = jax.ShapeDtypeStruct((ROWS, WIDTH), bf16)
@@ -483,7 +502,7 @@
     parts = pl.pallas_call(
         functools.partial(kernel, bits),
         out_shape=(rows, rows) + tuple(jax.ShapeDtypeStruct((n, HALF), bf16) for n in size),
-        in_specs=[vmem] * 7 + [smem, vmem],
+        in_specs=[whole, vmem, whole, whole, whole, whole, vmem, smem, whole],
         out_specs=(vmem,) * (2 + ng),
         scratch_shapes=scratch,
         compiler_params=pltpu.CompilerParams(

time: 66.2 us -> 65.9 us (level)
  no operation moved by 1% of the time
where the time goes in v5:
time: 65.9 us; the launch traced here: 65.8 us
  Pallas kernels  65.1 us (99%)
    pallas_call x1, Pallas kernels, local(): pl.pallas_call(functools.partial(kernel, bits), out_shape=(rows, rows) +...  62.4 us
    pallas_call x1, Pallas kernels, local(): pl.pallas_call(finish, out_shape=(rows, rows, square, square, square, squ...  2.78 us

profile of v5, /device:TPU:1, one launch (start us, length us, event | category | flops | bytes accessed | tf_op | source)
XLA Modules:
  0.0 65.8 jit_solution(17092667640143233946)
XLA Ops:
  0.6 62.4 %shard_map.144 = (bf16[512,256]{1,0:T(8,128)(2,1)}, bf16[512,256]{1,0:T(8,128)(2,1)}, bf16[1536,128]{1,0:T(8,128)(2,1)}, bf16[512,128]{1,0:T(8,128)(2,1)}) custom-call(bf16[512,256]{1,0:T(8,128)(2,1)} %bitcast.7, f32[1,256]{1,0:T(1,128)} %bitcast.9, bf16[256,256]{1,0:T(8,128)(2,1)} %refs_5_.3, bf16[256,256]{1,0:T(8,128)(2,1)} %refs_6_.1, ...), custom_call_target="tpu_custom_call" | custom-call | tf_op jit(solution)/shard_map/pallas_call | solution.py:502
  63.0 2.8 %shard_map.145 = (bf16[512,256]{1,0:T(8,128)(2,1)}, bf16[512,256]{1,0:T(8,128)(2,1)}, f32[256,256]{1,0:T(8,128)}, f32[256,256]{1,0:T(8,128)}, f32[256,256]{1,0:T...) custom-call(bf16[512,256]{1,0:T(8,128)(2,1)} %get-tuple-element.18.refs_0_, bf16[512,256]{1,0:T(8,128)(2,1)} %get-tuple-element.19.refs_1_, ...), custom_call_target="tpu_custom_call" | custom-call | tf_op jit(solution)/shard_map/pallas_call | solution.py:515
